TPU v7x, 512 devices: a whole 4x4x16 slice. The times are simulated.
512 devices in a mesh: freq: 64 (over z_lo, x, core), lat: 8 (over z_hi, y).
Axes of the slice: x: 4, y: 4, z: 16 (z_hi: 2, z_lo: 8; z = z_hi * 8 + z_lo), core: 2. Of those that a mesh axis runs over, the one named last changes fastest.
Arguments:
- frequencies: float32 [64], P('freq'), may hold values from 0.3 to 1.5
- slowness: float32 [2, 128, 1024], P(None, 'lat', 'freq'), may hold values from 0.5 to 1.5
- src_field: float32 [64, 2, 128, 1024], P('freq', None, 'lat'), may hold values from -6 to 6
- rec_field: float32 [64, 2, 128, 1024], P('freq', None, 'lat'), may hold values from -6 to 6
Outputs:
- depth_image: float32 [2, 128, 1024], P(None, 'lat', 'freq')
- src_final: float32 [64, 2, 128, 1024], P('freq', None, 'lat')
- rec_final: float32 [64, 2, 128, 1024], P('freq', None, 'lat')
All inputs are finite; a program needn't handle non-finite values.
Results may differ from a plain program's by a relative error of at most 0.0003.
Values sent between devices are 32-bit elements; how exact they have to be, the bound alone decides.
A program may use at most 64 MiB of HBM per device.

v0:
```python
import math
import jax
import jax.numpy as jnp
from jax import lax
from jax.sharding import PartitionSpec as P

NZ = 2
TERMS = 8
step_ratio = 1.0
damping = 0.1


def extended(block, sides, width):
    for axis, dim in sides:
        count = lax.axis_size(axis)
        forward = [(i, i + 1) for i in range(count - 1)]
        backward = [(target, source) for source, target in forward]
        low = lax.ppermute(
            lax.slice_in_dim(block, block.shape[dim] - width, None, axis=dim), axis, forward
        )
        high = lax.ppermute(lax.slice_in_dim(block, 0, width, axis=dim), axis, backward)
        block = jnp.concatenate([low, block, high], axis=dim)
    return block


def neighbours(values):
    zero_col = jnp.zeros_like(values[..., :1])
    from_right = jnp.concatenate([values[..., 1:], zero_col], axis=-1)
    from_left = jnp.concatenate([zero_col, values[..., :-1]], axis=-1)
    return from_right + from_left


def mcclellan(padded):
    centre = padded[..., 1:-1, :]
    vertical = padded[..., 2:, :] + padded[..., :-2, :]
    return -0.5 * centre + 0.25 * vertical + neighbours(0.25 * centre + 0.125 * vertical)


def coefficients(wavenum, term_count):
    angles = math.pi * (jnp.arange(term_count, dtype=jnp.float32) + 0.5) / term_count
    view_shape = (term_count,) + (1,) * wavenum.ndim
    node_angles = angles.reshape(view_shape)
    excess = wavenum[None] ** 2 - node_angles**2
    absorb = damping * wavenum[None] ** 2
    modulus = jnp.sqrt(excess * excess + absorb * absorb)
    larger = jnp.sqrt(0.5 * (modulus + jnp.abs(excess)))
    smaller = absorb / (2.0 * larger)
    propagating = excess >= 0
    real_part = jnp.where(propagating, larger, smaller)
    imag_part = jnp.where(propagating, smaller, larger)
    attenuation = jnp.exp(-step_ratio * imag_part)
    phase_re = attenuation * jnp.cos(step_ratio * real_part)
    phase_im = attenuation * jnp.sin(step_ratio * real_part)
    orders = jnp.arange(term_count, dtype=jnp.float32)
    weights = jnp.where(orders == 0, 1.0, 2.0) / term_count
    cosine_table = weights[:, None] * jnp.cos(orders[:, None] * angles[None, :])
    coef_re = jnp.einsum("nj,j...->n...", cosine_table, phase_re, precision=lax.Precision.HIGHEST)
    coef_im = jnp.einsum("nj,j...->n...", cosine_table, phase_im, precision=lax.Precision.HIGHEST)
    return (coef_re, coef_im)


def accumulate(summed, coef_re, coef_im, level):
    src_re = level[..., 0, :, :]
    src_im = level[..., 1, :, :]
    rec_re = level[..., 2, :, :]
    rec_im = level[..., 3, :, :]
    term = jnp.stack(
        [
            coef_re * src_re - coef_im * src_im,
            coef_re * src_im + coef_im * src_re,
            coef_re * rec_re + coef_im * rec_im,
            coef_re * rec_im - coef_im * rec_re,
        ],
        axis=-3,
    )
    return summed + term


def raise_level(values):
    padded = extended(values, (("lat", 2),), 1)
    return mcclellan(padded)


def rim_step(wavefields, coef_re, coef_im):
    term_count = coef_re.shape[0]
    previous = wavefields
    summed = accumulate(jnp.zeros_like(wavefields), coef_re[0], coef_im[0], previous)
    current = raise_level(previous)
    summed = accumulate(summed, coef_re[1], coef_im[1], current)
    for term_index in range(2, term_count):
        following = 2.0 * raise_level(current) - previous
        summed = accumulate(summed, coef_re[term_index], coef_im[term_index], following)
        previous, current = (current, following)
    return summed


def shards(frequencies, slowness, src_field, rec_field):
    wavefields = jnp.concatenate([src_field, rec_field], axis=1)
    freq_count = lax.axis_size("freq")
    norm_factor = 1.0 / math.sqrt(wavefields.shape[0] * freq_count)
    full_slow = lax.all_gather(slowness, "freq", axis=2, tiled=True)
    partials = []
    for depth_step in range(NZ):
        slow_layer = full_slow[depth_step]
        coef_re, coef_im = coefficients(frequencies[:, None, None] * slow_layer[None], TERMS)
        wavefields = rim_step(wavefields, coef_re, coef_im)
        partial_value = jnp.sum(
            wavefields[:, 0] * wavefields[:, 2] + wavefields[:, 1] * wavefields[:, 3], axis=0
        )
        partials.append(partial_value)
    depth_image = (
        lax.psum_scatter(jnp.stack(partials), "freq", scatter_dimension=2, tiled=True) * norm_factor
    )
    return (depth_image, wavefields[:, :2], wavefields[:, 2:])


def solution(mesh):
    placed = (
        P("freq"),
        P(None, "lat", "freq"),
        P("freq", None, "lat", None),
        P("freq", None, "lat", None),
    )
    return jax.shard_map(
        shards,
        mesh=mesh,
        in_specs=placed,
        out_specs=(
            P(None, "lat", "freq"),
            P("freq", None, "lat", None),
            P("freq", None, "lat", None),
        ),
        check_vma=False,
    )
```

profile of v0, /device:TPU:8, one launch (start us, length us, event | category | flops | bytes accessed | tf_op | source)
XLA Modules:
  0.0 897.7 jit_solution(5849739694801983435)
XLA Ops:
  9.5 7.7 collective-permute-start
  20.6 124.5 %all_gather.3 = f32[2,16,1024]{1,0,2:T(2,128)S(1)} all-gather(f32[2,16,16]{1,0,2:T(2,128)S(1)} %copy.34), channel_id=1, replica_groups=mesh['freq'=64,'lat'=8] {'freq'}, dimensions={2}, use_global_device_ids=true | all-gather | bytes 133120 | tf_op jit(solution)/shard_map/all_gather | solution.py:101
  146.6 2.8 fusion.27
  149.4 2.8 fusion.24
  152.3 2.8 fusion.21
  155.3 2.8 fusion.18
  160.1 2.4 collective-permute-start.2
  162.5 3.5 collective-permute-start.3
  171.8 13.0 %collective-permute-start.5 = (f32[1,4,1,1024]{3,0,2,1:T(1,128)S(1)}, f32[1,4,1,1024]{3,0,2,1:T(1,128)S(1)}, u32[]{:S(2)}, u32[]{:S(2)}) collective-permute-start(f32[1,4,1,1024]{3,0,2,1:T(1,128)S(1)} %get-tuple-element.133), channel_id=1, source_target_pairs={{0,1},{1,2},{2,3},{3,4},{4,5},{5,6},{6,7},{8,9},{9,10},{10,11},{11... | collective-permute-start | bytes 49160 | tf_op jit(solution)/shard_map/ppermute | solution.py:18
  190.1 14.7 %collective-permute-start.7 = (f32[1,4,1,1024]{3,0,2,1:T(1,128)S(1)}, f32[1,4,1,1024]{3,0,2,1:T(1,128)S(1)}, u32[]{:S(2)}, u32[]{:S(2)}) collective-permute-start(f32[1,4,1,1024]{3,0,2,1:T(1,128)S(1)} %get-tuple-element.129), channel_id=1, source_target_pairs={{0,1},{1,2},{2,3},{3,4},{4,5},{5,6},{6,7},{8,9},{9,10},{10,11},{11... | collective-permute-start | bytes 49160 | tf_op jit(solution)/shard_map/ppermute | solution.py:18
  210.1 14.9 %collective-permute-start.9 = (f32[1,4,1,1024]{3,0,2,1:T(1,128)S(1)}, f32[1,4,1,1024]{3,0,2,1:T(1,128)S(1)}, u32[]{:S(2)}, u32[]{:S(2)}) collective-permute-start(f32[1,4,1,1024]{3,0,2,1:T(1,128)S(1)} %get-tuple-element.125), channel_id=1, source_target_pairs={{0,1},{1,2},{2,3},{3,4},{4,5},{5,6},{6,7},{8,9},{9,10},{10,11},{11... | collective-permute-start | bytes 49160 | tf_op jit(solution)/shard_map/ppermute | solution.py:18
  230.2 15.3 %collective-permute-start.11 = (f32[1,4,1,1024]{3,0,2,1:T(1,128)S(1)}, f32[1,4,1,1024]{3,0,2,1:T(1,128)S(1)}, u32[]{:S(2)}, u32[]{:S(2)}) collective-permute-start(f32[1,4,1,1024]{3,0,2,1:T(1,128)S(1)} %get-tuple-element.121), channel_id=1, source_target_pairs={{0,1},{1,2},{2,3},{3,4},{4,5},{5,6},{6,7},{8,9},{9,10},{10,11},{11... | collective-permute-start | bytes 49160 | tf_op jit(solution)/shard_map/ppermute | solution.py:18
  250.8 14.9 %collective-permute-start.13 = (f32[1,4,1,1024]{3,0,2,1:T(1,128)S(1)}, f32[1,4,1,1024]{3,0,2,1:T(1,128)S(1)}, u32[]{:S(2)}, u32[]{:S(2)}) collective-permute-start(f32[1,4,1,1024]{3,0,2,1:T(1,128)S(1)} %get-tuple-element.117), channel_id=1, source_target_pairs={{0,1},{1,2},{2,3},{3,4},{4,5},{5,6},{6,7},{8,9},{9,10},{10,11},{11... | collective-permute-start | bytes 49160 | tf_op jit(solution)/shard_map/ppermute | solution.py:18
  274.0 14.9 %collective-permute-start.15 = (f32[1,4,1,1024]{3,0,2,1:T(1,128)S(1)}, f32[1,4,1,1024]{3,0,2,1:T(1,128)S(1)}, u32[]{:S(2)}, u32[]{:S(2)}) collective-permute-start(f32[1,4,1,1024]{3,0,2,1:T(1,128)S(1)} %get-tuple-element.113), channel_id=1, source_target_pairs={{0,1},{1,2},{2,3},{3,4},{4,5},{5,6},{6,7},{8,9},{9,10},{10,11},{11... | collective-permute-start | bytes 49160 | tf_op jit(solution)/shard_map/ppermute | solution.py:18
  294.0 14.7 %collective-permute-start.17 = (f32[1,4,1,1024]{3,0,2,1:T(1,128)S(1)}, f32[1,4,1,1024]{3,0,2,1:T(1,128)S(1)}, u32[]{:S(2)}, u32[]{:S(2)}) collective-permute-start(f32[1,4,1,1024]{3,0,2,1:T(1,128)S(1)} %get-tuple-element.109), channel_id=1, source_target_pairs={{0,1},{1,2},{2,3},{3,4},{4,5},{5,6},{6,7},{8,9},{9,10},{10,11},{11... | collective-permute-start | bytes 49160 | tf_op jit(solution)/shard_map/ppermute | solution.py:18
  311.1 3.3 multiply_subtract_fusion.5
  316.3 14.9 %collective-permute-start.19 = (f32[1,4,1,1024]{3,0,2,1:T(1,128)S(1)}, f32[1,4,1,1024]{3,0,2,1:T(1,128)S(1)}, u32[]{:S(2)}, u32[]{:S(2)}) collective-permute-start(f32[1,4,1,1024]{3,0,2,1:T(1,128)S(1)} %get-tuple-element.105), channel_id=1, source_target_pairs={{0,1},{1,2},{2,3},{3,4},{4,5},{5,6},{6,7},{8,9},{9,10},{10,11},{11... | collective-permute-start | bytes 49160 | tf_op jit(solution)/shard_map/ppermute | solution.py:18
  336.4 15.2 %collective-permute-start.21 = (f32[1,4,1,1024]{3,0,2,1:T(1,128)S(1)}, f32[1,4,1,1024]{3,0,2,1:T(1,128)S(1)}, u32[]{:S(2)}, u32[]{:S(2)}) collective-permute-start(f32[1,4,1,1024]{3,0,2,1:T(1,128)S(1)} %get-tuple-element.101), channel_id=1, source_target_pairs={{0,1},{1,2},{2,3},{3,4},{4,5},{5,6},{6,7},{8,9},{9,10},{10,11},{11... | collective-permute-start | bytes 49160 | tf_op jit(solution)/shard_map/ppermute | solution.py:18
  356.6 15.0 %collective-permute-start.23 = (f32[1,4,1,1024]{3,0,2,1:T(1,128)S(1)}, f32[1,4,1,1024]{3,0,2,1:T(1,128)S(1)}, u32[]{:S(2)}, u32[]{:S(2)}) collective-permute-start(f32[1,4,1,1024]{3,0,2,1:T(1,128)S(1)} %get-tuple-element.97), channel_id=1, source_target_pairs={{0,1},{1,2},{2,3},{3,4},{4,5},{5,6},{6,7},{8,9},{9,10},{10,11},{11... | collective-permute-start | bytes 49160 | tf_op jit(solution)/shard_map/ppermute | solution.py:18
  376.8 15.0 %collective-permute-start.25 = (f32[1,4,1,1024]{3,0,2,1:T(1,128)S(1)}, f32[1,4,1,1024]{3,0,2,1:T(1,128)S(1)}, u32[]{:S(2)}, u32[]{:S(2)}) collective-permute-start(f32[1,4,1,1024]{3,0,2,1:T(1,128)S(1)} %get-tuple-element.93), channel_id=1, source_target_pairs={{0,1},{1,2},{2,3},{3,4},{4,5},{5,6},{6,7},{8,9},{9,10},{10,11},{11... | collective-permute-start | bytes 49160 | tf_op jit(solution)/shard_map/ppermute | solution.py:18
  397.0 15.0 %collective-permute-start.27 = (f32[1,4,1,1024]{3,0,2,1:T(1,128)S(1)}, f32[1,4,1,1024]{3,0,2,1:T(1,128)S(1)}, u32[]{:S(2)}, u32[]{:S(2)}) collective-permute-start(f32[1,4,1,1024]{3,0,2,1:T(1,128)S(1)} %get-tuple-element.89), channel_id=1, source_target_pairs={{0,1},{1,2},{2,3},{3,4},{4,5},{5,6},{6,7},{8,9},{9,10},{10,11},{11... | collective-permute-start | bytes 49160 | tf_op jit(solution)/shard_map/ppermute | solution.py:18
  417.2 5.9 copy.46
  423.2 7.1 reshape.1693
  431.6 457.5 %reduce-scatter.4.cloned.1.call-done = f32[16,32]{1,0:T(8,128)} async-done(((f32[1024,32]{1,0:T(8,128)}), f32[16,32]{1,0:T(8,128)}) %reduce-scatter.4.cloned.1.call-update) | async-done | bytes 2064
  (141 shorter events, 81.0 us)
Async XLA Ops:
  7.2 881.9 %reduce-scatter.4.cloned.1.call-start = ((), (), s32[]{:S(2)}) async-start(), calls=%async_computation.1 | async-start | bytes 532480
  9.5 148.7 %collective-permute-start = (f32[1,4,1,1024]{3,0,2,1:T(1,128)S(1)}, f32[1,4,1,1024]{3,0,2,1:T(1,128)S(1)}, u32[]{:S(2)}, u32[]{:S(2)}) collective-permute-start(f32[1,4,1,1024]{3,0,2,1:T(1,128)S(1)} %get-tuple-element.140), channel_id=1, source_target_pairs={{1,0},{2,1},{3,2},{4,3},{5,4},{6,5},{7,6},{9,8},{10,9},{11,10},{12... | collective-permute-start | bytes 49160 | tf_op jit(solution)/shard_map/ppermute | solution.py:21
  17.2 140.9 %collective-permute-start.1 = (f32[1,4,1,1024]{3,0,2,1:T(1,128)S(1)}, f32[1,4,1,1024]{3,0,2,1:T(1,128)S(1)}, u32[]{:S(2)}, u32[]{:S(2)}) collective-permute-start(f32[1,4,1,1024]{3,0,2,1:T(1,128)S(1)} %get-tuple-element.141), channel_id=1, source_target_pairs={{0,1},{1,2},{2,3},{3,4},{4,5},{5,6},{6,7},{8,9},{9,10},{10,11},{11... | collective-permute-start | bytes 49160 | tf_op jit(solution)/shard_map/ppermute | solution.py:18
  169.9 16.5 %collective-permute-start.4 = (f32[1,4,1,1024]{3,0,2,1:T(1,128)S(1)}, f32[1,4,1,1024]{3,0,2,1:T(1,128)S(1)}, u32[]{:S(2)}, u32[]{:S(2)}) collective-permute-start(f32[1,4,1,1024]{3,0,2,1:T(1,128)S(1)} %get-tuple-element.132), channel_id=1, source_target_pairs={{1,0},{2,1},{3,2},{4,3},{5,4},{6,5},{7,6},{9,8},{10,9},{11,10},{12... | collective-permute-start | bytes 49160 | tf_op jit(solution)/shard_map/ppermute | solution.py:21
  188.2 18.2 %collective-permute-start.6 = (f32[1,4,1,1024]{3,0,2,1:T(1,128)S(1)}, f32[1,4,1,1024]{3,0,2,1:T(1,128)S(1)}, u32[]{:S(2)}, u32[]{:S(2)}) collective-permute-start(f32[1,4,1,1024]{3,0,2,1:T(1,128)S(1)} %get-tuple-element.128), channel_id=1, source_target_pairs={{1,0},{2,1},{3,2},{4,3},{5,4},{6,5},{7,6},{9,8},{10,9},{11,10},{12... | collective-permute-start | bytes 49160 | tf_op jit(solution)/shard_map/ppermute | solution.py:21
  208.2 18.3 %collective-permute-start.8 = (f32[1,4,1,1024]{3,0,2,1:T(1,128)S(1)}, f32[1,4,1,1024]{3,0,2,1:T(1,128)S(1)}, u32[]{:S(2)}, u32[]{:S(2)}) collective-permute-start(f32[1,4,1,1024]{3,0,2,1:T(1,128)S(1)} %get-tuple-element.124), channel_id=1, source_target_pairs={{1,0},{2,1},{3,2},{4,3},{5,4},{6,5},{7,6},{9,8},{10,9},{11,10},{12... | collective-permute-start | bytes 49160 | tf_op jit(solution)/shard_map/ppermute | solution.py:21
  210.1 16.4 %collective-permute-start.9 = (f32[1,4,1,1024]{3,0,2,1:T(1,128)S(1)}, f32[1,4,1,1024]{3,0,2,1:T(1,128)S(1)}, u32[]{:S(2)}, u32[]{:S(2)}) collective-permute-start(f32[1,4,1,1024]{3,0,2,1:T(1,128)S(1)} %get-tuple-element.125), channel_id=1, source_target_pairs={{0,1},{1,2},{2,3},{3,4},{4,5},{5,6},{6,7},{8,9},{9,10},{10,11},{11... | collective-permute-start | bytes 49160 | tf_op jit(solution)/shard_map/ppermute | solution.py:18
  228.3 18.8 %collective-permute-start.10 = (f32[1,4,1,1024]{3,0,2,1:T(1,128)S(1)}, f32[1,4,1,1024]{3,0,2,1:T(1,128)S(1)}, u32[]{:S(2)}, u32[]{:S(2)}) collective-permute-start(f32[1,4,1,1024]{3,0,2,1:T(1,128)S(1)} %get-tuple-element.120), channel_id=1, source_target_pairs={{1,0},{2,1},{3,2},{4,3},{5,4},{6,5},{7,6},{9,8},{10,9},{11,10},{12... | collective-permute-start | bytes 49160 | tf_op jit(solution)/shard_map/ppermute | solution.py:21
  230.2 16.8 %collective-permute-start.11 = (f32[1,4,1,1024]{3,0,2,1:T(1,128)S(1)}, f32[1,4,1,1024]{3,0,2,1:T(1,128)S(1)}, u32[]{:S(2)}, u32[]{:S(2)}) collective-permute-start(f32[1,4,1,1024]{3,0,2,1:T(1,128)S(1)} %get-tuple-element.121), channel_id=1, source_target_pairs={{0,1},{1,2},{2,3},{3,4},{4,5},{5,6},{6,7},{8,9},{9,10},{10,11},{11... | collective-permute-start | bytes 49160 | tf_op jit(solution)/shard_map/ppermute | solution.py:18
  248.9 18.4 %collective-permute-start.12 = (f32[1,4,1,1024]{3,0,2,1:T(1,128)S(1)}, f32[1,4,1,1024]{3,0,2,1:T(1,128)S(1)}, u32[]{:S(2)}, u32[]{:S(2)}) collective-permute-start(f32[1,4,1,1024]{3,0,2,1:T(1,128)S(1)} %get-tuple-element.116), channel_id=1, source_target_pairs={{1,0},{2,1},{3,2},{4,3},{5,4},{6,5},{7,6},{9,8},{10,9},{11,10},{12... | collective-permute-start | bytes 49160 | tf_op jit(solution)/shard_map/ppermute | solution.py:21
  250.8 16.4 %collective-permute-start.13 = (f32[1,4,1,1024]{3,0,2,1:T(1,128)S(1)}, f32[1,4,1,1024]{3,0,2,1:T(1,128)S(1)}, u32[]{:S(2)}, u32[]{:S(2)}) collective-permute-start(f32[1,4,1,1024]{3,0,2,1:T(1,128)S(1)} %get-tuple-element.117), channel_id=1, source_target_pairs={{0,1},{1,2},{2,3},{3,4},{4,5},{5,6},{6,7},{8,9},{9,10},{10,11},{11... | collective-permute-start | bytes 49160 | tf_op jit(solution)/shard_map/ppermute | solution.py:18
  272.0 17.2 %collective-permute-start.14 = (f32[1,4,1,1024]{3,0,2,1:T(1,128)S(1)}, f32[1,4,1,1024]{3,0,2,1:T(1,128)S(1)}, u32[]{:S(2)}, u32[]{:S(2)}) collective-permute-start(f32[1,4,1,1024]{3,0,2,1:T(1,128)S(1)} %get-tuple-element.112), channel_id=1, source_target_pairs={{1,0},{2,1},{3,2},{4,3},{5,4},{6,5},{7,6},{9,8},{10,9},{11,10},{12... | collective-permute-start | bytes 49160 | tf_op jit(solution)/shard_map/ppermute | solution.py:21
  274.0 16.4 %collective-permute-start.15 = (f32[1,4,1,1024]{3,0,2,1:T(1,128)S(1)}, f32[1,4,1,1024]{3,0,2,1:T(1,128)S(1)}, u32[]{:S(2)}, u32[]{:S(2)}) collective-permute-start(f32[1,4,1,1024]{3,0,2,1:T(1,128)S(1)} %get-tuple-element.113), channel_id=1, source_target_pairs={{0,1},{1,2},{2,3},{3,4},{4,5},{5,6},{6,7},{8,9},{9,10},{10,11},{11... | collective-permute-start | bytes 49160 | tf_op jit(solution)/shard_map/ppermute | solution.py:18
  292.0 17.0 %collective-permute-start.16 = (f32[1,4,1,1024]{3,0,2,1:T(1,128)S(1)}, f32[1,4,1,1024]{3,0,2,1:T(1,128)S(1)}, u32[]{:S(2)}, u32[]{:S(2)}) collective-permute-start(f32[1,4,1,1024]{3,0,2,1:T(1,128)S(1)} %get-tuple-element.108), channel_id=1, source_target_pairs={{1,0},{2,1},{3,2},{4,3},{5,4},{6,5},{7,6},{9,8},{10,9},{11,10},{12... | collective-permute-start | bytes 49160 | tf_op jit(solution)/shard_map/ppermute | solution.py:21
  314.4 17.2 %collective-permute-start.18 = (f32[1,4,1,1024]{3,0,2,1:T(1,128)S(1)}, f32[1,4,1,1024]{3,0,2,1:T(1,128)S(1)}, u32[]{:S(2)}, u32[]{:S(2)}) collective-permute-start(f32[1,4,1,1024]{3,0,2,1:T(1,128)S(1)} %get-tuple-element.104), channel_id=1, source_target_pairs={{1,0},{2,1},{3,2},{4,3},{5,4},{6,5},{7,6},{9,8},{10,9},{11,10},{12... | collective-permute-start | bytes 49160 | tf_op jit(solution)/shard_map/ppermute | solution.py:21
  316.3 16.4 %collective-permute-start.19 = (f32[1,4,1,1024]{3,0,2,1:T(1,128)S(1)}, f32[1,4,1,1024]{3,0,2,1:T(1,128)S(1)}, u32[]{:S(2)}, u32[]{:S(2)}) collective-permute-start(f32[1,4,1,1024]{3,0,2,1:T(1,128)S(1)} %get-tuple-element.105), channel_id=1, source_target_pairs={{0,1},{1,2},{2,3},{3,4},{4,5},{5,6},{6,7},{8,9},{9,10},{10,11},{11... | collective-permute-start | bytes 49160 | tf_op jit(solution)/shard_map/ppermute | solution.py:18
  334.5 17.4 %collective-permute-start.20 = (f32[1,4,1,1024]{3,0,2,1:T(1,128)S(1)}, f32[1,4,1,1024]{3,0,2,1:T(1,128)S(1)}, u32[]{:S(2)}, u32[]{:S(2)}) collective-permute-start(f32[1,4,1,1024]{3,0,2,1:T(1,128)S(1)} %get-tuple-element.100), channel_id=1, source_target_pairs={{1,0},{2,1},{3,2},{4,3},{5,4},{6,5},{7,6},{9,8},{10,9},{11,10},{12... | collective-permute-start | bytes 49160 | tf_op jit(solution)/shard_map/ppermute | solution.py:21
  336.4 16.5 %collective-permute-start.21 = (f32[1,4,1,1024]{3,0,2,1:T(1,128)S(1)}, f32[1,4,1,1024]{3,0,2,1:T(1,128)S(1)}, u32[]{:S(2)}, u32[]{:S(2)}) collective-permute-start(f32[1,4,1,1024]{3,0,2,1:T(1,128)S(1)} %get-tuple-element.101), channel_id=1, source_target_pairs={{0,1},{1,2},{2,3},{3,4},{4,5},{5,6},{6,7},{8,9},{9,10},{10,11},{11... | collective-permute-start | bytes 49160 | tf_op jit(solution)/shard_map/ppermute | solution.py:18
  354.7 17.3 %collective-permute-start.22 = (f32[1,4,1,1024]{3,0,2,1:T(1,128)S(1)}, f32[1,4,1,1024]{3,0,2,1:T(1,128)S(1)}, u32[]{:S(2)}, u32[]{:S(2)}) collective-permute-start(f32[1,4,1,1024]{3,0,2,1:T(1,128)S(1)} %get-tuple-element.96), channel_id=1, source_target_pairs={{1,0},{2,1},{3,2},{4,3},{5,4},{6,5},{7,6},{9,8},{10,9},{11,10},{12... | collective-permute-start | bytes 49160 | tf_op jit(solution)/shard_map/ppermute | solution.py:21
  356.6 16.5 %collective-permute-start.23 = (f32[1,4,1,1024]{3,0,2,1:T(1,128)S(1)}, f32[1,4,1,1024]{3,0,2,1:T(1,128)S(1)}, u32[]{:S(2)}, u32[]{:S(2)}) collective-permute-start(f32[1,4,1,1024]{3,0,2,1:T(1,128)S(1)} %get-tuple-element.97), channel_id=1, source_target_pairs={{0,1},{1,2},{2,3},{3,4},{4,5},{5,6},{6,7},{8,9},{9,10},{10,11},{11... | collective-permute-start | bytes 49160 | tf_op jit(solution)/shard_map/ppermute | solution.py:18
  374.9 17.3 %collective-permute-start.24 = (f32[1,4,1,1024]{3,0,2,1:T(1,128)S(1)}, f32[1,4,1,1024]{3,0,2,1:T(1,128)S(1)}, u32[]{:S(2)}, u32[]{:S(2)}) collective-permute-start(f32[1,4,1,1024]{3,0,2,1:T(1,128)S(1)} %get-tuple-element.92), channel_id=1, source_target_pairs={{1,0},{2,1},{3,2},{4,3},{5,4},{6,5},{7,6},{9,8},{10,9},{11,10},{12... | collective-permute-start | bytes 49160 | tf_op jit(solution)/shard_map/ppermute | solution.py:21
  376.8 16.5 %collective-permute-start.25 = (f32[1,4,1,1024]{3,0,2,1:T(1,128)S(1)}, f32[1,4,1,1024]{3,0,2,1:T(1,128)S(1)}, u32[]{:S(2)}, u32[]{:S(2)}) collective-permute-start(f32[1,4,1,1024]{3,0,2,1:T(1,128)S(1)} %get-tuple-element.93), channel_id=1, source_target_pairs={{0,1},{1,2},{2,3},{3,4},{4,5},{5,6},{6,7},{8,9},{9,10},{10,11},{11... | collective-permute-start | bytes 49160 | tf_op jit(solution)/shard_map/ppermute | solution.py:18
  395.1 17.3 %collective-permute-start.26 = (f32[1,4,1,1024]{3,0,2,1:T(1,128)S(1)}, f32[1,4,1,1024]{3,0,2,1:T(1,128)S(1)}, u32[]{:S(2)}, u32[]{:S(2)}) collective-permute-start(f32[1,4,1,1024]{3,0,2,1:T(1,128)S(1)} %get-tuple-element.88), channel_id=1, source_target_pairs={{1,0},{2,1},{3,2},{4,3},{5,4},{6,5},{7,6},{9,8},{10,9},{11,10},{12... | collective-permute-start | bytes 49160 | tf_op jit(solution)/shard_map/ppermute | solution.py:21
  397.0 16.5 %collective-permute-start.27 = (f32[1,4,1,1024]{3,0,2,1:T(1,128)S(1)}, f32[1,4,1,1024]{3,0,2,1:T(1,128)S(1)}, u32[]{:S(2)}, u32[]{:S(2)}) collective-permute-start(f32[1,4,1,1024]{3,0,2,1:T(1,128)S(1)} %get-tuple-element.89), channel_id=1, source_target_pairs={{0,1},{1,2},{2,3},{3,4},{4,5},{5,6},{6,7},{8,9},{9,10},{10,11},{11... | collective-permute-start | bytes 49160 | tf_op jit(solution)/shard_map/ppermute | solution.py:18
  (7 other events, 90.2 us)
Sparse Core Ops, SparseCore 0:
  430.4 458.6 reduce-scatter.3
where the time goes:
time: 901 us; the launch traced here: 898 us
  waiting for transfers between devices  466 us (52%)
  starting transfers between devices  216 us (24%)
  blocking collectives  124 us (14%)
  other arithmetic  34.9 us (4%)
  local copies, waits for them, and re-layouts  29 us (3%)
  between operations  15.8 us (2%)
  matrix products  11.2 us (1%)
    unnamed x2, waiting for transfers between devices  457 us
    ppermute x14, starting transfers between devices, extended(): lax.ppermute(lax.slice_in_dim(block, block.shape[dim] - width, None, axis...  183 us
    all_gather x1, blocking collectives, shards(): full_slow = lax.all_gather(slowness, 'freq', axis=2, tiled=True)  124 us
    ppermute x14, starting transfers between devices, extended(): lax.ppermute(lax.slice_in_dim(block, 0, width, axis=dim), axis, backward)  33.1 us
    unnamed x16, local copies, waits for them, and re-layouts  19.6 us
  transfers between devices with their start and end apart: 29, of which 9 were waited for; matrix products, arithmetic and copies ran while one was open for 3% of the time, Pallas kernels for 0%

commit v1 on v0

--- a/solution.py
+++ b/solution.py
@@ -98,7 +98,9 @@
     wavefields = jnp.concatenate([src_field, rec_field], axis=1)
     freq_count = lax.axis_size("freq")
     norm_factor = 1.0 / math.sqrt(wavefields.shape[0] * freq_count)
-    full_slow = lax.all_gather(slowness, "freq", axis=2, tiled=True)
+    full_slow = jnp.concatenate(
+        lax.all_to_all(jnp.stack([slowness] * lax.axis_size("freq")), "freq", 0, 0), axis=2
+    )
     partials = []
     for depth_step in range(NZ):
         slow_layer = full_slow[depth_step]

time: 901 us -> 801 us (0.89)
  blocking collectives: 124 us -> 0 us
  waiting for transfers between devices: 466 us -> 478 us
  starting transfers between devices: 216 us -> 227 us
    all_gather x1 -> x0, blocking collectives: 124 us -> none  [shards(): full_slow = lax.all_gather(slowness, 'freq', axis=2, tiled=True)]
    all_to_all x0 -> x1, starting transfers between devices: none -> 15.4 us  [shards(): lax.all_to_all(jnp.stack([slowness] * lax.axis_size('freq')), 'freq', 0, 0)]
    ppermute x14, waiting for transfers between devices: 8.28 us -> 17.5 us  [extended(): lax.ppermute(lax.slice_in_dim(block, block.shape[dim] - width, None, axis...]
    unnamed x16 -> x15, local copies, waits for them, and re-layouts: 19.6 us -> 19.6 us
  transfers between devices with their start and end apart: 29 -> 30, of which waited for: 9 -> 14; matrix products, arithmetic and copies ran while one was open for 3% -> 1% of each run, Pallas kernels for 0% -> 0%
where the time goes in v1:
time: 801 us; the launch traced here: 791 us
  waiting for transfers between devices  478 us (60%)
  starting transfers between devices  227 us (28%)
  local copies, waits for them, and re-layouts  30.3 us (4%)
  other arithmetic  27.3 us (3%)
  between operations  15.8 us (2%)
  matrix products  12.4 us (2%)
    unnamed x2, waiting for transfers between devices  461 us
    ppermute x14, starting transfers between devices, extended(): lax.ppermute(lax.slice_in_dim(block, block.shape[dim] - width, None, axis...  179 us
    ppermute x14, starting transfers between devices, extended(): lax.ppermute(lax.slice_in_dim(block, 0, width, axis=dim), axis, backward)  32.7 us
    unnamed x15, local copies, waits for them, and re-layouts  19.6 us
    ppermute x14, waiting for transfers between devices, extended(): lax.ppermute(lax.slice_in_dim(block, block.shape[dim] - width, None, axis...  17.5 us
  transfers between devices with their start and end apart: 30, of which 14 were waited for; matrix products, arithmetic and copies ran while one was open for 1% of the time, Pallas kernels for 0%

profile of v1, /device:TPU:8, one launch (start us, length us, event | category | flops | bytes accessed | tf_op | source)
XLA Modules:
  0.0 791.3 jit_solution(13705648713179419107)
XLA Ops:
  9.4 7.7 collective-permute-start
  19.1 3.7 collective-permute-done.1
  26.4 3.9 collective-permute-start.3
  35.9 7.8 collective-permute-start.5
  48.8 15.0 %collective-permute-start.7 = (f32[1,4,1,1024]{3,0,2,1:T(1,128)S(1)}, f32[1,4,1,1024]{3,0,2,1:T(1,128)S(1)}, u32[]{:S(2)}, u32[]{:S(2)}) collective-permute-start(f32[1,4,1,1024]{3,0,2,1:T(1,128)S(1)} %get-tuple-element.128), channel_id=1, source_target_pairs={{0,1},{1,2},{2,3},{3,4},{4,5},{5,6},{6,7},{8,9},{9,10},{10,11},{11... | collective-permute-start | bytes 49160 | tf_op jit(solution)/shard_map/ppermute | solution.py:18
  69.0 15.0 %collective-permute-start.9 = (f32[1,4,1,1024]{3,0,2,1:T(1,128)S(1)}, f32[1,4,1,1024]{3,0,2,1:T(1,128)S(1)}, u32[]{:S(2)}, u32[]{:S(2)}) collective-permute-start(f32[1,4,1,1024]{3,0,2,1:T(1,128)S(1)} %get-tuple-element.124), channel_id=1, source_target_pairs={{0,1},{1,2},{2,3},{3,4},{4,5},{5,6},{6,7},{8,9},{9,10},{10,11},{11... | collective-permute-start | bytes 49160 | tf_op jit(solution)/shard_map/ppermute | solution.py:18
  85.2 15.4 %all-to-all-start = ((f32[64,1,512]{2,1,0:T(1,128)}), f32[64,1,512]{2,1,0:T(1,128)S(1)}, u32[]{:S(2)}, u32[]{:S(2)}) async-start(f32[64,1,512]{2,1,0:T(1,128)} %reshape.1718), calls=%async_computation | async-start | bytes 262144 | tf_op jit(solution)/shard_map/all_to_all | solution.py:102
  104.4 15.2 %collective-permute-start.11 = (f32[1,4,1,1024]{3,0,2,1:T(1,128)S(1)}, f32[1,4,1,1024]{3,0,2,1:T(1,128)S(1)}, u32[]{:S(2)}, u32[]{:S(2)}) collective-permute-start(f32[1,4,1,1024]{3,0,2,1:T(1,128)S(1)} %get-tuple-element.120), channel_id=1, source_target_pairs={{0,1},{1,2},{2,3},{3,4},{4,5},{5,6},{6,7},{8,9},{9,10},{10,11},{11... | collective-permute-start | bytes 49160 | tf_op jit(solution)/shard_map/ppermute | solution.py:18
  124.6 15.0 %collective-permute-start.13 = (f32[1,4,1,1024]{3,0,2,1:T(1,128)S(1)}, f32[1,4,1,1024]{3,0,2,1:T(1,128)S(1)}, u32[]{:S(2)}, u32[]{:S(2)}) collective-permute-start(f32[1,4,1,1024]{3,0,2,1:T(1,128)S(1)} %get-tuple-element.116), channel_id=1, source_target_pairs={{0,1},{1,2},{2,3},{3,4},{4,5},{5,6},{6,7},{8,9},{9,10},{10,11},{11... | collective-permute-start | bytes 49160 | tf_op jit(solution)/shard_map/ppermute | solution.py:18
  145.8 2.8 fusion.18
  148.6 4.0 fusion.21
  153.1 2.8 fusion.24
  155.9 2.8 fusion.27
  164.3 15.2 %collective-permute-start.15 = (f32[1,4,1,1024]{3,0,2,1:T(1,128)S(1)}, f32[1,4,1,1024]{3,0,2,1:T(1,128)S(1)}, u32[]{:S(2)}, u32[]{:S(2)}) collective-permute-start(f32[1,4,1,1024]{3,0,2,1:T(1,128)S(1)} %get-tuple-element.112), channel_id=1, source_target_pairs={{0,1},{1,2},{2,3},{3,4},{4,5},{5,6},{6,7},{8,9},{9,10},{10,11},{11... | collective-permute-start | bytes 49160 | tf_op jit(solution)/shard_map/ppermute | solution.py:18
  184.1 15.0 %collective-permute-start.17 = (f32[1,4,1,1024]{3,0,2,1:T(1,128)S(1)}, f32[1,4,1,1024]{3,0,2,1:T(1,128)S(1)}, u32[]{:S(2)}, u32[]{:S(2)}) collective-permute-start(f32[1,4,1,1024]{3,0,2,1:T(1,128)S(1)} %get-tuple-element.108), channel_id=1, source_target_pairs={{0,1},{1,2},{2,3},{3,4},{4,5},{5,6},{6,7},{8,9},{9,10},{10,11},{11... | collective-permute-start | bytes 49160 | tf_op jit(solution)/shard_map/ppermute | solution.py:18
  201.5 3.3 multiply_subtract_fusion.5
  206.8 15.0 %collective-permute-start.19 = (f32[1,4,1,1024]{3,0,2,1:T(1,128)S(1)}, f32[1,4,1,1024]{3,0,2,1:T(1,128)S(1)}, u32[]{:S(2)}, u32[]{:S(2)}) collective-permute-start(f32[1,4,1,1024]{3,0,2,1:T(1,128)S(1)} %get-tuple-element.104), channel_id=1, source_target_pairs={{0,1},{1,2},{2,3},{3,4},{4,5},{5,6},{6,7},{8,9},{9,10},{10,11},{11... | collective-permute-start | bytes 49160 | tf_op jit(solution)/shard_map/ppermute | solution.py:18
  227.0 15.0 %collective-permute-start.21 = (f32[1,4,1,1024]{3,0,2,1:T(1,128)S(1)}, f32[1,4,1,1024]{3,0,2,1:T(1,128)S(1)}, u32[]{:S(2)}, u32[]{:S(2)}) collective-permute-start(f32[1,4,1,1024]{3,0,2,1:T(1,128)S(1)} %get-tuple-element.100), channel_id=1, source_target_pairs={{0,1},{1,2},{2,3},{3,4},{4,5},{5,6},{6,7},{8,9},{9,10},{10,11},{11... | collective-permute-start | bytes 49160 | tf_op jit(solution)/shard_map/ppermute | solution.py:18
  247.1 15.0 %collective-permute-start.23 = (f32[1,4,1,1024]{3,0,2,1:T(1,128)S(1)}, f32[1,4,1,1024]{3,0,2,1:T(1,128)S(1)}, u32[]{:S(2)}, u32[]{:S(2)}) collective-permute-start(f32[1,4,1,1024]{3,0,2,1:T(1,128)S(1)} %get-tuple-element.96), channel_id=1, source_target_pairs={{0,1},{1,2},{2,3},{3,4},{4,5},{5,6},{6,7},{8,9},{9,10},{10,11},{11... | collective-permute-start | bytes 49160 | tf_op jit(solution)/shard_map/ppermute | solution.py:18
  267.3 15.2 %collective-permute-start.25 = (f32[1,4,1,1024]{3,0,2,1:T(1,128)S(1)}, f32[1,4,1,1024]{3,0,2,1:T(1,128)S(1)}, u32[]{:S(2)}, u32[]{:S(2)}) collective-permute-start(f32[1,4,1,1024]{3,0,2,1:T(1,128)S(1)} %get-tuple-element.92), channel_id=1, source_target_pairs={{0,1},{1,2},{2,3},{3,4},{4,5},{5,6},{6,7},{8,9},{9,10},{10,11},{11... | collective-permute-start | bytes 49160 | tf_op jit(solution)/shard_map/ppermute | solution.py:18
  287.5 15.0 %collective-permute-start.27 = (f32[1,4,1,1024]{3,0,2,1:T(1,128)S(1)}, f32[1,4,1,1024]{3,0,2,1:T(1,128)S(1)}, u32[]{:S(2)}, u32[]{:S(2)}) collective-permute-start(f32[1,4,1,1024]{3,0,2,1:T(1,128)S(1)} %get-tuple-element.88), channel_id=1, source_target_pairs={{0,1},{1,2},{2,3},{3,4},{4,5},{5,6},{6,7},{8,9},{9,10},{10,11},{11... | collective-permute-start | bytes 49160 | tf_op jit(solution)/shard_map/ppermute | solution.py:18
  307.7 5.9 copy.48
  313.7 7.1 reshape.1716
  322.2 460.6 %reduce-scatter.4.cloned.1.call-done = f32[16,32]{1,0:T(8,128)} async-done(((f32[1024,32]{1,0:T(8,128)}), f32[16,32]{1,0:T(8,128)}) %reduce-scatter.4.cloned.1.call-update) | async-done | bytes 2064
  (148 shorter events, 82.1 us)
Async XLA Ops:
  46.9 17.0 %collective-permute-start.6 = (f32[1,4,1,1024]{3,0,2,1:T(1,128)S(1)}, f32[1,4,1,1024]{3,0,2,1:T(1,128)S(1)}, u32[]{:S(2)}, u32[]{:S(2)}) collective-permute-start(f32[1,4,1,1024]{3,0,2,1:T(1,128)S(1)} %get-tuple-element.127), channel_id=1, source_target_pairs={{1,0},{2,1},{3,2},{4,3},{5,4},{6,5},{7,6},{9,8},{10,9},{11,10},{12... | collective-permute-start | bytes 49160 | tf_op jit(solution)/shard_map/ppermute | solution.py:21
  48.8 16.5 %collective-permute-start.7 = (f32[1,4,1,1024]{3,0,2,1:T(1,128)S(1)}, f32[1,4,1,1024]{3,0,2,1:T(1,128)S(1)}, u32[]{:S(2)}, u32[]{:S(2)}) collective-permute-start(f32[1,4,1,1024]{3,0,2,1:T(1,128)S(1)} %get-tuple-element.128), channel_id=1, source_target_pairs={{0,1},{1,2},{2,3},{3,4},{4,5},{5,6},{6,7},{8,9},{9,10},{10,11},{11... | collective-permute-start | bytes 49160 | tf_op jit(solution)/shard_map/ppermute | solution.py:18
  67.1 33.6 %collective-permute-start.8 = (f32[1,4,1,1024]{3,0,2,1:T(1,128)S(1)}, f32[1,4,1,1024]{3,0,2,1:T(1,128)S(1)}, u32[]{:S(2)}, u32[]{:S(2)}) collective-permute-start(f32[1,4,1,1024]{3,0,2,1:T(1,128)S(1)} %get-tuple-element.123), channel_id=1, source_target_pairs={{1,0},{2,1},{3,2},{4,3},{5,4},{6,5},{7,6},{9,8},{10,9},{11,10},{12... | collective-permute-start | bytes 49160 | tf_op jit(solution)/shard_map/ppermute | solution.py:21
  69.0 31.7 %collective-permute-start.9 = (f32[1,4,1,1024]{3,0,2,1:T(1,128)S(1)}, f32[1,4,1,1024]{3,0,2,1:T(1,128)S(1)}, u32[]{:S(2)}, u32[]{:S(2)}) collective-permute-start(f32[1,4,1,1024]{3,0,2,1:T(1,128)S(1)} %get-tuple-element.124), channel_id=1, source_target_pairs={{0,1},{1,2},{2,3},{3,4},{4,5},{5,6},{6,7},{8,9},{9,10},{10,11},{11... | collective-permute-start | bytes 49160 | tf_op jit(solution)/shard_map/ppermute | solution.py:18
  85.2 57.6 %all-to-all-start = ((f32[64,1,512]{2,1,0:T(1,128)}), f32[64,1,512]{2,1,0:T(1,128)S(1)}, u32[]{:S(2)}, u32[]{:S(2)}) async-start(f32[64,1,512]{2,1,0:T(1,128)} %reshape.1718), calls=%async_computation | async-start | bytes 262144 | tf_op jit(solution)/shard_map/all_to_all | solution.py:102
  100.6 682.1 %reduce-scatter.4.cloned.1.call-start = ((), (), s32[]{:S(2)}) async-start(), calls=%async_computation.2 | async-start | bytes 532480
  102.4 17.2 %collective-permute-start.10 = (f32[1,4,1,1024]{3,0,2,1:T(1,128)S(1)}, f32[1,4,1,1024]{3,0,2,1:T(1,128)S(1)}, u32[]{:S(2)}, u32[]{:S(2)}) collective-permute-start(f32[1,4,1,1024]{3,0,2,1:T(1,128)S(1)} %get-tuple-element.119), channel_id=1, source_target_pairs={{1,0},{2,1},{3,2},{4,3},{5,4},{6,5},{7,6},{9,8},{10,9},{11,10},{12... | collective-permute-start | bytes 49160 | tf_op jit(solution)/shard_map/ppermute | solution.py:21
  104.4 16.5 %collective-permute-start.11 = (f32[1,4,1,1024]{3,0,2,1:T(1,128)S(1)}, f32[1,4,1,1024]{3,0,2,1:T(1,128)S(1)}, u32[]{:S(2)}, u32[]{:S(2)}) collective-permute-start(f32[1,4,1,1024]{3,0,2,1:T(1,128)S(1)} %get-tuple-element.120), channel_id=1, source_target_pairs={{0,1},{1,2},{2,3},{3,4},{4,5},{5,6},{6,7},{8,9},{9,10},{10,11},{11... | collective-permute-start | bytes 49160 | tf_op jit(solution)/shard_map/ppermute | solution.py:18
  122.6 17.6 %collective-permute-start.12 = (f32[1,4,1,1024]{3,0,2,1:T(1,128)S(1)}, f32[1,4,1,1024]{3,0,2,1:T(1,128)S(1)}, u32[]{:S(2)}, u32[]{:S(2)}) collective-permute-start(f32[1,4,1,1024]{3,0,2,1:T(1,128)S(1)} %get-tuple-element.115), channel_id=1, source_target_pairs={{1,0},{2,1},{3,2},{4,3},{5,4},{6,5},{7,6},{9,8},{10,9},{11,10},{12... | collective-permute-start | bytes 49160 | tf_op jit(solution)/shard_map/ppermute | solution.py:21
  124.6 16.5 %collective-permute-start.13 = (f32[1,4,1,1024]{3,0,2,1:T(1,128)S(1)}, f32[1,4,1,1024]{3,0,2,1:T(1,128)S(1)}, u32[]{:S(2)}, u32[]{:S(2)}) collective-permute-start(f32[1,4,1,1024]{3,0,2,1:T(1,128)S(1)} %get-tuple-element.116), channel_id=1, source_target_pairs={{0,1},{1,2},{2,3},{3,4},{4,5},{5,6},{6,7},{8,9},{9,10},{10,11},{11... | collective-permute-start | bytes 49160 | tf_op jit(solution)/shard_map/ppermute | solution.py:18
  162.4 17.5 %collective-permute-start.14 = (f32[1,4,1,1024]{3,0,2,1:T(1,128)S(1)}, f32[1,4,1,1024]{3,0,2,1:T(1,128)S(1)}, u32[]{:S(2)}, u32[]{:S(2)}) collective-permute-start(f32[1,4,1,1024]{3,0,2,1:T(1,128)S(1)} %get-tuple-element.111), channel_id=1, source_target_pairs={{1,0},{2,1},{3,2},{4,3},{5,4},{6,5},{7,6},{9,8},{10,9},{11,10},{12... | collective-permute-start | bytes 49160 | tf_op jit(solution)/shard_map/ppermute | solution.py:21
  164.3 16.2 %collective-permute-start.15 = (f32[1,4,1,1024]{3,0,2,1:T(1,128)S(1)}, f32[1,4,1,1024]{3,0,2,1:T(1,128)S(1)}, u32[]{:S(2)}, u32[]{:S(2)}) collective-permute-start(f32[1,4,1,1024]{3,0,2,1:T(1,128)S(1)} %get-tuple-element.112), channel_id=1, source_target_pairs={{0,1},{1,2},{2,3},{3,4},{4,5},{5,6},{6,7},{8,9},{9,10},{10,11},{11... | collective-permute-start | bytes 49160 | tf_op jit(solution)/shard_map/ppermute | solution.py:18
  182.2 17.2 %collective-permute-start.16 = (f32[1,4,1,1024]{3,0,2,1:T(1,128)S(1)}, f32[1,4,1,1024]{3,0,2,1:T(1,128)S(1)}, u32[]{:S(2)}, u32[]{:S(2)}) collective-permute-start(f32[1,4,1,1024]{3,0,2,1:T(1,128)S(1)} %get-tuple-element.107), channel_id=1, source_target_pairs={{1,0},{2,1},{3,2},{4,3},{5,4},{6,5},{7,6},{9,8},{10,9},{11,10},{12... | collective-permute-start | bytes 49160 | tf_op jit(solution)/shard_map/ppermute | solution.py:21
  184.1 16.5 %collective-permute-start.17 = (f32[1,4,1,1024]{3,0,2,1:T(1,128)S(1)}, f32[1,4,1,1024]{3,0,2,1:T(1,128)S(1)}, u32[]{:S(2)}, u32[]{:S(2)}) collective-permute-start(f32[1,4,1,1024]{3,0,2,1:T(1,128)S(1)} %get-tuple-element.108), channel_id=1, source_target_pairs={{0,1},{1,2},{2,3},{3,4},{4,5},{5,6},{6,7},{8,9},{9,10},{10,11},{11... | collective-permute-start | bytes 49160 | tf_op jit(solution)/shard_map/ppermute | solution.py:18
  204.9 17.3 %collective-permute-start.18 = (f32[1,4,1,1024]{3,0,2,1:T(1,128)S(1)}, f32[1,4,1,1024]{3,0,2,1:T(1,128)S(1)}, u32[]{:S(2)}, u32[]{:S(2)}) collective-permute-start(f32[1,4,1,1024]{3,0,2,1:T(1,128)S(1)} %get-tuple-element.103), channel_id=1, source_target_pairs={{1,0},{2,1},{3,2},{4,3},{5,4},{6,5},{7,6},{9,8},{10,9},{11,10},{12... | collective-permute-start | bytes 49160 | tf_op jit(solution)/shard_map/ppermute | solution.py:21
  206.8 16.5 %collective-permute-start.19 = (f32[1,4,1,1024]{3,0,2,1:T(1,128)S(1)}, f32[1,4,1,1024]{3,0,2,1:T(1,128)S(1)}, u32[]{:S(2)}, u32[]{:S(2)}) collective-permute-start(f32[1,4,1,1024]{3,0,2,1:T(1,128)S(1)} %get-tuple-element.104), channel_id=1, source_target_pairs={{0,1},{1,2},{2,3},{3,4},{4,5},{5,6},{6,7},{8,9},{9,10},{10,11},{11... | collective-permute-start | bytes 49160 | tf_op jit(solution)/shard_map/ppermute | solution.py:18
  225.0 17.3 %collective-permute-start.20 = (f32[1,4,1,1024]{3,0,2,1:T(1,128)S(1)}, f32[1,4,1,1024]{3,0,2,1:T(1,128)S(1)}, u32[]{:S(2)}, u32[]{:S(2)}) collective-permute-start(f32[1,4,1,1024]{3,0,2,1:T(1,128)S(1)} %get-tuple-element.99), channel_id=1, source_target_pairs={{1,0},{2,1},{3,2},{4,3},{5,4},{6,5},{7,6},{9,8},{10,9},{11,10},{12... | collective-permute-start | bytes 49160 | tf_op jit(solution)/shard_map/ppermute | solution.py:21
  227.0 16.5 %collective-permute-start.21 = (f32[1,4,1,1024]{3,0,2,1:T(1,128)S(1)}, f32[1,4,1,1024]{3,0,2,1:T(1,128)S(1)}, u32[]{:S(2)}, u32[]{:S(2)}) collective-permute-start(f32[1,4,1,1024]{3,0,2,1:T(1,128)S(1)} %get-tuple-element.100), channel_id=1, source_target_pairs={{0,1},{1,2},{2,3},{3,4},{4,5},{5,6},{6,7},{8,9},{9,10},{10,11},{11... | collective-permute-start | bytes 49160 | tf_op jit(solution)/shard_map/ppermute | solution.py:18
  245.2 17.3 %collective-permute-start.22 = (f32[1,4,1,1024]{3,0,2,1:T(1,128)S(1)}, f32[1,4,1,1024]{3,0,2,1:T(1,128)S(1)}, u32[]{:S(2)}, u32[]{:S(2)}) collective-permute-start(f32[1,4,1,1024]{3,0,2,1:T(1,128)S(1)} %get-tuple-element.95), channel_id=1, source_target_pairs={{1,0},{2,1},{3,2},{4,3},{5,4},{6,5},{7,6},{9,8},{10,9},{11,10},{12... | collective-permute-start | bytes 49160 | tf_op jit(solution)/shard_map/ppermute | solution.py:21
  247.1 16.5 %collective-permute-start.23 = (f32[1,4,1,1024]{3,0,2,1:T(1,128)S(1)}, f32[1,4,1,1024]{3,0,2,1:T(1,128)S(1)}, u32[]{:S(2)}, u32[]{:S(2)}) collective-permute-start(f32[1,4,1,1024]{3,0,2,1:T(1,128)S(1)} %get-tuple-element.96), channel_id=1, source_target_pairs={{0,1},{1,2},{2,3},{3,4},{4,5},{5,6},{6,7},{8,9},{9,10},{10,11},{11... | collective-permute-start | bytes 49160 | tf_op jit(solution)/shard_map/ppermute | solution.py:18
  265.4 17.4 %collective-permute-start.24 = (f32[1,4,1,1024]{3,0,2,1:T(1,128)S(1)}, f32[1,4,1,1024]{3,0,2,1:T(1,128)S(1)}, u32[]{:S(2)}, u32[]{:S(2)}) collective-permute-start(f32[1,4,1,1024]{3,0,2,1:T(1,128)S(1)} %get-tuple-element.91), channel_id=1, source_target_pairs={{1,0},{2,1},{3,2},{4,3},{5,4},{6,5},{7,6},{9,8},{10,9},{11,10},{12... | collective-permute-start | bytes 49160 | tf_op jit(solution)/shard_map/ppermute | solution.py:21
  267.3 16.5 %collective-permute-start.25 = (f32[1,4,1,1024]{3,0,2,1:T(1,128)S(1)}, f32[1,4,1,1024]{3,0,2,1:T(1,128)S(1)}, u32[]{:S(2)}, u32[]{:S(2)}) collective-permute-start(f32[1,4,1,1024]{3,0,2,1:T(1,128)S(1)} %get-tuple-element.92), channel_id=1, source_target_pairs={{0,1},{1,2},{2,3},{3,4},{4,5},{5,6},{6,7},{8,9},{9,10},{10,11},{11... | collective-permute-start | bytes 49160 | tf_op jit(solution)/shard_map/ppermute | solution.py:18
  285.6 17.3 %collective-permute-start.26 = (f32[1,4,1,1024]{3,0,2,1:T(1,128)S(1)}, f32[1,4,1,1024]{3,0,2,1:T(1,128)S(1)}, u32[]{:S(2)}, u32[]{:S(2)}) collective-permute-start(f32[1,4,1,1024]{3,0,2,1:T(1,128)S(1)} %get-tuple-element.87), channel_id=1, source_target_pairs={{1,0},{2,1},{3,2},{4,3},{5,4},{6,5},{7,6},{9,8},{10,9},{11,10},{12... | collective-permute-start | bytes 49160 | tf_op jit(solution)/shard_map/ppermute | solution.py:21
  287.5 16.5 %collective-permute-start.27 = (f32[1,4,1,1024]{3,0,2,1:T(1,128)S(1)}, f32[1,4,1,1024]{3,0,2,1:T(1,128)S(1)}, u32[]{:S(2)}, u32[]{:S(2)}) collective-permute-start(f32[1,4,1,1024]{3,0,2,1:T(1,128)S(1)} %get-tuple-element.88), channel_id=1, source_target_pairs={{0,1},{1,2},{2,3},{3,4},{4,5},{5,6},{6,7},{8,9},{9,10},{10,11},{11... | collective-permute-start | bytes 49160 | tf_op jit(solution)/shard_map/ppermute | solution.py:18
  (8 other events, 149.1 us)
Sparse Core Ops, SparseCore 0:
  320.9 461.7 reduce-scatter.3
